TPU v7x, 32 devices: a whole 2x2x4 slice. The times are simulated.
32 devices in a mesh: grp: 2 (over x), tmpl: 8 (over z, y), tm: 2 (over core).
Axes of the slice: x: 2, y: 2, z: 4, core: 2. Of those that a mesh axis runs over, the one named last changes fastest.
Arguments:
- spectra: bfloat16 [1024, 4, 8192], P(('grp', 'tm', 'tmpl')), parts along dimension 0, may hold values from -6 to 6
- offsets: int32 [1024, 16], P(('grp', 'tm'), 'tmpl'), parts along dimension 0, may hold values from 0 to 1008
- fractions: float32 [4096], P(('grp', 'tmpl')), parts along dimension 0, may hold values from 0.1 to 0.9
- antenna: float32 [1024, 4], P('grp'), parts along dimension 0, may hold values from -2 to 2, as said below
- starts: int32 [64], P('grp'), parts along dimension 0, may hold values from 0 to 255
- durations: int32 [64], P('grp'), parts along dimension 0, may hold values from 48 to 256
Outputs:
- fstat_map: float32 [32, 32, 4096], P('tm', None, ('grp', 'tmpl')), parts along dimension 2
- loudest: float32 [64, 32], P(('grp', 'tm')), parts along dimension 0
There are 2 independent parts, one for each index of `grp`. A program takes and returns all parts, laid end to end along the dimension named above; each array names one. Nothing has to cross between parts.
Inputs may be any that keep to these rules, and one draw needn't show every extreme that they name: `antenna`: each detector's responses a and b turn once every 48 SFTs with magnitudes that vary from SFT to SFT.
All inputs are finite; a program needn't handle non-finite values.
Results may differ from a plain program's by a relative error of at most 0.0051.
Values may be sent and summed in bfloat16 or wider, within the bound.
No kernel may reach another device: no remote copies, remote signals or barrier semaphores. Data moves between devices by JAX's collectives and lax.ppermute only.
A program may use at most 128 MiB of HBM per device.

v0:
```python
import jax
import jax.numpy as jnp
from jax import lax
from jax.sharding import PartitionSpec as P

W = 16


def weigh(windows, antenna):
    values = windows.astype(jnp.float32)
    detector_one = values[:, 0:2]
    detector_two = values[:, 2:4]
    weighted_a = (
        antenna[:, 0][:, None, None, None] * detector_one
        + antenna[:, 1][:, None, None, None] * detector_two
    )
    weighted_b = (
        antenna[:, 2][:, None, None, None] * detector_one
        + antenna[:, 3][:, None, None, None] * detector_two
    )
    return jnp.concatenate([weighted_a, weighted_b], axis=1).astype(jnp.bfloat16)


def dirichlet(fractions):
    bin_shift = jnp.arange(W, dtype=jnp.float32)
    distance = fractions[:, None] + (W // 2 - 1) - bin_shift[None, :]
    parity = (jnp.arange(W, dtype=jnp.int32) % 2).astype(jnp.float32)
    alternate = 1.0 - 2.0 * parity
    return (alternate[None, :] * jnp.sin(jnp.pi * fractions)[:, None] / (jnp.pi * distance)).astype(
        jnp.bfloat16
    )


def antenna_prefix(antenna):
    along_a = antenna[:, 0] * antenna[:, 0] + antenna[:, 1] * antenna[:, 1]
    along_b = antenna[:, 2] * antenna[:, 2] + antenna[:, 3] * antenna[:, 3]
    across = antenna[:, 0] * antenna[:, 2] + antenna[:, 1] * antenna[:, 3]
    stacked = jnp.stack([along_a, along_b, across], axis=1)
    return jnp.concatenate([jnp.zeros((1, 3), jnp.float32), jnp.cumsum(stacked, axis=0)], axis=0)


def statistic(interval, weights):
    real_a = interval[..., 0, :]
    imag_a = interval[..., 1, :]
    real_b = interval[..., 2, :]
    imag_b = interval[..., 3, :]
    weight_a = weights[..., 0:1]
    weight_b = weights[..., 1:2]
    weight_c = weights[..., 2:3]
    numerator = (
        weight_b * (real_a * real_a + imag_a * imag_a)
        + weight_a * (real_b * real_b + imag_b * imag_b)
        - 2.0 * weight_c * (real_a * real_b + imag_a * imag_b)
    )
    return numerator / (weight_a * weight_b - weight_c * weight_c)


def selector(places, band_width):
    bin_ids = jnp.arange(band_width, dtype=jnp.int32)
    return (places[..., None] == bin_ids).astype(jnp.bfloat16)


def body(spectra, offsets, fractions, antenna, starts, durations):
    block_count = offsets.shape[1]
    template_count = fractions.shape[0]
    block_width = template_count // block_count
    window_shift = jnp.arange(W, dtype=jnp.int32)
    band_count = lax.axis_size("tmpl")
    band_width = spectra.shape[2] // band_count
    owned_offsets = lax.all_to_all(offsets, "tmpl", split_axis=0, concat_axis=1, tiled=True)
    owned_rows = owned_offsets.shape[0]
    all_blocks = owned_offsets.shape[1]
    places = (owned_offsets[:, :, None] + window_shift[None, None, :]).reshape(
        owned_rows, band_count, block_count * W
    )
    picker = selector(places, band_width)
    split_bands = spectra.reshape(owned_rows, 4, band_count, band_width)
    chosen = jnp.einsum("sctn,stkn->stck", split_bands, picker, preferred_element_type=jnp.float32)
    chosen = chosen.astype(jnp.bfloat16).reshape(owned_rows, band_count, 4, block_count, W)
    flat_windows = jnp.transpose(chosen, (0, 2, 1, 3, 4)).reshape(owned_rows, 4, all_blocks * W)
    arrived = lax.all_to_all(flat_windows, "tmpl", split_axis=2, concat_axis=0, tiled=True)
    windows = arrived.reshape(arrived.shape[0], 4, block_count, W)
    sft_rows = windows.shape[0]
    time_block = lax.axis_index("tm")
    first_sft = time_block * sft_rows
    local_antenna = lax.dynamic_slice_in_dim(antenna, first_sft, sft_rows, 0)
    weighted = weigh(windows, local_antenna)
    kernel = dirichlet(fractions).reshape(block_count, block_width, W)
    atom_rows = jnp.einsum("scbm,bqm->sbcq", weighted, kernel, preferred_element_type=jnp.float32)
    feature_count = block_count * 4 * block_width
    atom_rows = atom_rows.reshape(sft_rows, feature_count)
    grid_size = starts.shape[0]
    my_rows = grid_size // lax.axis_size("tm")
    my_durations = lax.dynamic_slice_in_dim(durations, time_block * my_rows, my_rows, 0)
    end_points = starts[None, :] + my_durations[:, None]
    sft_global = first_sft + jnp.arange(sft_rows, dtype=jnp.int32)
    before_mask = (sft_global[None, :] < starts[:, None]).astype(jnp.float32)
    before = jnp.dot(before_mask, atom_rows, precision=lax.Precision.HIGHEST)
    chosen_ends = starts[None, :] + durations[:, None]
    through_mask = (sft_global[None, None, :] < chosen_ends[:, :, None]).astype(jnp.float32)
    through_mask = through_mask.reshape(my_rows * lax.axis_size("tm") * grid_size, sft_rows)
    through_end = jnp.dot(through_mask, atom_rows, precision=lax.Precision.HIGHEST)
    interval = lax.psum_scatter(
        through_end.reshape(my_rows * lax.axis_size("tm"), grid_size, feature_count) - before[None],
        "tm",
        scatter_dimension=0,
        tiled=True,
    )
    cum_weights = antenna_prefix(antenna)
    weights = cum_weights[end_points] - cum_weights[starts][None]
    split_interval = interval.reshape(my_rows, grid_size, block_count, 4, block_width)
    fstat_blocks = statistic(split_interval, weights[:, :, None, :])
    fstat_map = fstat_blocks.reshape(my_rows, grid_size, template_count)
    loudest = lax.pmax(jnp.max(fstat_map, axis=2), "tmpl")
    return (fstat_map, loudest)


def solution(mesh):
    in_specs = (
        P(("grp", "tm", "tmpl"), None, None),
        P(("grp", "tm"), "tmpl"),
        P(("grp", "tmpl")),
        P("grp", None),
        P("grp"),
        P("grp"),
    )
    out_specs = (P("tm", None, ("grp", "tmpl")), P(("grp", "tm"), None))
    return jax.shard_map(body, mesh=mesh, in_specs=in_specs, out_specs=out_specs, check_vma=False)
```

profile of v0, /device:TPU:0, one launch (start us, length us, event | category | flops | bytes accessed | tf_op | source)
XLA Modules:
  0.0 116.5 jit_solution(2259706734415102542)
XLA Ops:
  7.2 0.9 all_to_all.9
  8.1 0.6 copy.26
  8.7 7.3 %all-to-all-start = ((s32[8,32,2]{1,2,0:T(2,128)}), s32[8,32,2]{1,2,0:T(2,128)S(1)}, u32[]{:S(2)}, u32[]{:S(2)}) async-start(s32[8,32,2]{1,2,0:T(2,128)} %copy.26), calls=%async_computation | async-start | bytes 16384 | tf_op jit(solution)/shard_map/all_to_all | solution.py:70
  16.0 0.7 sine_bitcast_fusion
  16.7 0.7 broadcast_add_fusion
  17.5 5.0 %all-to-all-done = s32[8,32,2]{1,2,0:T(2,128)S(1)} async-done(((s32[8,32,2]{1,2,0:T(2,128)}), s32[8,32,2]{1,2,0:T(2,128)S(1)}, u32[]{:S(2)}, u32[]{:S(2)}) %all-to-all-start) | async-done | bytes 2080 | tf_op jit(solution)/shard_map/all_to_all | solution.py:70
  22.7 7.1 %fusion.3 = bf16[32,8,4,32]{3,2,1,0:T(4,128)(2,1)S(1)} fusion(bf16[32,4,8,1024]{3,1,2,0:T(4,128)(2,1)S(1)} %bitcast.67, s32[32,8,32]{2,1,0:T(8,128)S(1)} %copy.27), kind=kOutput, calls=%fused_computation.7 | convolution fusion | flops 75530240 | bytes 2195456 | tf_op jit(solution)/shard_map/sctn,stkn->stck/dot_general | solution.py:78
  30.3 0.9 reshape.267
  31.2 3.4 %all-to-all-start.1 = ((bf16[8,2,2048]{2,1,0:T(2,128)(2,1)}), bf16[8,2,2048]{2,1,0:T(2,128)(2,1)S(1)}, u32[]{:S(2)}, u32[]{:S(2)}) async-start(bf16[8,2,2048]{2,1,0:T(2,128)(2,1)} %reshape.267), calls=%async_computation.1 | async-start | bytes 131072 | tf_op jit(solution)/shard_map/all_to_all | solution.py:81
  34.8 6.7 %all-to-all-done.1 = bf16[8,2,2048]{2,1,0:T(2,128)(2,1)S(1)} async-done(((bf16[8,2,2048]{2,1,0:T(2,128)(2,1)}), bf16[8,2,2048]{2,1,0:T(2,128)(2,1)S(1)}, u32[]{:S(2)}, u32[]{:S(2)}) %all-to-all-start.1) | async-done | bytes 65568 | tf_op jit(solution)/shard_map/all_to_all | solution.py:81
  42.5 0.6 fusion.12
  43.1 3.8 %convolution_subtract_fusion = f32[32,32,1024]{2,1,0:T(8,128)} fusion(f32[256,1024,1]{0,1,2:T(8,128)S(1)} %bitcast.69, f32[32,1024]{1,0:T(8,128)S(1)} %fusion.12, s32[32,32]{1,0:T(8,128)S(1)} %broadcast_add_fusion, s32[256]{0:T(256)S(1)} %iota_add_fusion), kind=kOutput, calls=%fused_computation.5 | convolution fusion | flops 3222536192 | bytes 5379072 | tf_op jit(solution)/shard_map/dot_general | solution.py:102
  47.0 0.9 reduce-window.6
  48.8 1.0 gather_fusion
  50.1 0.6 gather_fusion.1
  50.7 5.9 %reduce-scatter.2.cloned.1.call-done = f32[16,32,1024]{2,1,0:T(8,128)} async-done(((f32[32,32,1024]{2,1,0:T(8,128)}), f32[16,32,1024]{2,1,0:T(8,128)}) %reduce-scatter.2.cloned.1.call-update) | async-done | bytes 2097168 | tf_op jit(solution)/shard_map/reduce_scatter | solution.py:103
  56.7 3.2 %reshape.219 = f32[16,32,2,4,128]{4,3,2,1,0:T(4,128)} reshape(f32[16,32,1024]{2,1,0:T(8,128)} %reduce-scatter.2.cloned.1.call-done) | data formatting | bytes 4194304 | tf_op jit(solution)/shard_map/reshape | solution.py:111
  59.9 6.7 %multiply_add_fusion.2 = (f32[16,32,2,1,128]{4,3,2,1,0:T(1,128)S(1)}, f32[16,32,2,1,128]{4,3,2,1,0:T(1,128)S(1)}, f32[16,32,2,1,128]{4,3,2,1,0:T(1,128)}) fusion(f32[16,32,2,4,128]{4,3,2,1,0:T(4,128)} %reshape.219), kind=kLoop, calls=%fused_computation.14 | loop fusion | flops 1179648 | bytes 3670016 | tf_op jit(solution)/shard_map/add | solution.py:51
  67.1 12.7 %fusion.7 = (f32[16,32]{1,0:T(8,128)S(1)}, f32[16,32,2,128]{3,2,1,0:T(2,128)}, f32[16,32,2,128]{3,2,1,0:T(2,128)}, f32[16,32,2,128]{3,2,1,0:T(2,128)}) fusion(f32[16,32,2,1,128]{4,3,2,1,0:T(1,128)S(1)} %get-tuple-element.7, f32[16,32,2,1,128]{4,3,2,1,0:T(1,128)} %get-tuple-element.8, f32[16,32,2,1,128]{4,3,2,1,0:T(1,128)S(1)} %get-tuple-element.6, ...), kind=kLoop, calls=%fused_computation.17 | loop fusion | flops 916992 | bytes 3155972 | tf_op jit(solution)/shard_map/reduce_max | solution.py:114
  79.8 1.5 %add.201 = f32[16,32,256]{2,1,0:T(8,128)S(1)} reshape(f32[16,32,2,128]{3,2,1,0:T(2,128)} %get-tuple-element.3) | data formatting | bytes 1048576 | tf_op jit(solution)/shard_map/add | solution.py:51
  81.3 1.5 %add.203 = f32[16,32,256]{2,1,0:T(8,128)S(1)} reshape(f32[16,32,2,128]{3,2,1,0:T(2,128)} %get-tuple-element.4) | data formatting | bytes 1048576 | tf_op jit(solution)/shard_map/add | solution.py:52
  82.7 2.3 %add.206 = f32[16,32,256]{2,1,0:T(8,128)} reshape(f32[16,32,2,128]{3,2,1,0:T(2,128)} %get-tuple-element.5) | data formatting | bytes 1048576 | tf_op jit(solution)/shard_map/add | solution.py:53
  85.0 22.5 %pmax.7 = f32[16,32]{1,0:T(8,128)} all-reduce(f32[16,32]{1,0:T(8,128)S(1)} %get-tuple-element.2), channel_id=1, replica_groups=mesh['grp'=2,'tmpl'=8,'tm'=2] {'tmpl'}, use_global_device_ids=true, to_apply=%region_4.5 | all-reduce | flops 512 | bytes 4096 | tf_op jit(solution)/shard_map/pmax | solution.py:114
  107.5 2.2 %subtract_divide_fusion.1 = f32[16,32,256]{2,1,0:T(8,128)} fusion(f32[16,32,256]{2,1,0:T(8,128)} %add.206, f32[16,32,256]{2,1,0:T(8,128)S(1)} %add.203, f32[16,32,256]{2,1,0:T(8,128)S(1)} %add.201, f32[16,32]{1,0:T(8,128)S(1)} %get-tuple-element.14, f32[16,32]{1,0:T(8,128)S(1)} %get-tuple-element.15, f32[16,32]{1,0:T(8,128)S(1)} %get-tuple-element.16, ...), kind=kLoop, calls=%fused_computation.11 | loop fusion | flops 786432 | bytes 2105344 | tf_op jit(solution)/shard_map/div | solution.py:55
  (45 shorter events, 3.6 us)
Async XLA Ops:
  7.2 15.5 %copy-start = (bf16[32,4,8192]{2,1,0:T(4,128)(2,1)S(1)}, bf16[32,4,8192]{2,1,0:T(4,128)(2,1)}, u32[]{:S(2)}) copy-start(bf16[32,4,8192]{2,1,0:T(4,128)(2,1)} %param.6) | copy-start | bytes 6291460
  8.7 13.8 %all-to-all-start = ((s32[8,32,2]{1,2,0:T(2,128)}), s32[8,32,2]{1,2,0:T(2,128)S(1)}, u32[]{:S(2)}, u32[]{:S(2)}) async-start(s32[8,32,2]{1,2,0:T(2,128)} %copy.26), calls=%async_computation | async-start | bytes 16384 | tf_op jit(solution)/shard_map/all_to_all | solution.py:70
  22.7 12.0 %copy-start.1 = (f32[512,4]{0,1:T(4,128)S(1)}, f32[512,4]{0,1:T(4,128)}, u32[]{:S(2)}) copy-start(f32[512,4]{0,1:T(4,128)} %param.9) | copy-start | bytes 24580
  29.8 12.7 %copy-start.2 = (s32[32]{0:T(128)S(1)}, s32[32]{0:T(128)}, u32[]{:S(2)}) copy-start(s32[32]{0:T(128)} %param.10) | copy-start | bytes 388
  31.2 10.2 %all-to-all-start.1 = ((bf16[8,2,2048]{2,1,0:T(2,128)(2,1)}), bf16[8,2,2048]{2,1,0:T(2,128)(2,1)S(1)}, u32[]{:S(2)}, u32[]{:S(2)}) async-start(bf16[8,2,2048]{2,1,0:T(2,128)(2,1)} %reshape.267), calls=%async_computation.1 | async-start | bytes 131072 | tf_op jit(solution)/shard_map/all_to_all | solution.py:81
  34.6 22.1 %reduce-scatter.2.cloned.1.call-start = ((), (), s32[]{:S(2)}) async-start(), calls=%async_computation.3 | async-start | bytes 6291456 | tf_op jit(solution)/shard_map/reduce_scatter | solution.py:103
  43.1 5.5 %copy-start.3 = (s32[32]{0:T(128)S(1)}, s32[32]{0:T(128)}, u32[]{:S(2)}) copy-start(s32[32]{0:T(128)} %param.11) | copy-start | bytes 388
Sparse Core Ops, SparseCore 0:
  47.1 9.5 reduce-scatter.1
where the time goes:
time: 117 us
  other arithmetic  24.5 us (21%)
  blocking collectives  22.5 us (19%)
  waiting for transfers between devices  17.6 us (15%)
  local copies, waits for them, and re-layouts  15.1 us (13%)
  between operations  14.2 us (12%)
  matrix products  11.9 us (10%)
  starting transfers between devices  10.7 us (9%)
    pmax x1, blocking collectives, body(): loudest = lax.pmax(jnp.max(fstat_map, axis=2), 'tmpl')  22.5 us
    reduce_max x1, other arithmetic, body(): loudest = lax.pmax(jnp.max(fstat_map, axis=2), 'tmpl')  12.7 us
    all_to_all x1, starting transfers between devices, body(): lax.all_to_all(offsets, 'tmpl', split_axis=0, concat_axis=1, tiled=True)  7.28 us
    dot_general x1, matrix products, body(): jnp.einsum('sctn,stkn->stck', split_bands, picker, preferred_element_type...  7.05 us
    all_to_all x1, waiting for transfers between devices, body(): lax.all_to_all(flat_windows, 'tmpl', split_axis=2, concat_axis=0, tiled=T...  6.68 us
    add x1, other arithmetic, statistic(): real_a * real_a + imag_a * imag_a  6.67 us
    reduce_scatter x1, waiting for transfers between devices, body(): lax.psum_scatter(through_end.reshape(my_rows * lax.axis_size('tm'), grid_...  5.92 us
    all_to_all x1, waiting for transfers between devices, body(): lax.all_to_all(offsets, 'tmpl', split_axis=0, concat_axis=1, tiled=True)  4.96 us
  transfers between devices with their start and end apart: 3, of which 3 were waited for; matrix products, arithmetic and copies ran while one was open for 5% of the time, Pallas kernels for 0%

commit v1 on v0

v1 whole, which is shorter than its diff:
```python
import functools

import jax
import jax.numpy as jnp
from jax import lax
from jax.experimental import pallas as pl
from jax.experimental.pallas import tpu as pltpu
from jax.sharding import PartitionSpec as P

W = 16
LANES = 128
NT = (((1,), (1,)), ((), ()))


def iota(shape, axis):
    return lax.broadcasted_iota(jnp.int32, shape, axis)


def pick_kernel(bands, rows, band_width, me_ref, *refs):
    offset_refs = refs[:bands]
    spec_ref, out_ref, high_ref, low_ref = refs[bands:]
    me = me_ref[0]
    blocks = offset_refs[0].shape[0]
    sft_count = offset_refs[0].shape[1]
    chunks = band_width // LANES
    offsets = jnp.concatenate([ref[...] for ref in offset_refs], axis=0)
    mine = iota((rows, sft_count), 1) == iota((rows, sft_count), 0) + me * rows
    mine = mine.astype(jnp.bfloat16)
    spread_shape = (bands * blocks, bands * LANES)
    source = iota(spread_shape, 0)
    target = iota(spread_shape, 1)
    wanted = ((source // blocks) ^ me) * blocks + source % blocks
    holds = (target // LANES) * blocks + (target // W) % blocks
    spread = (wanted == holds).astype(jnp.bfloat16)

    def lay_out(values, ref):
        own = lax.dot_general(mine, values.astype(jnp.float32).astype(jnp.bfloat16), NT, preferred_element_type=jnp.float32)
        ref[...] = jnp.dot(own.astype(jnp.bfloat16), spread, preferred_element_type=jnp.float32).astype(jnp.int32)

    lay_out(offsets // LANES, high_ref)
    lay_out(offsets % LANES, low_ref)
    lane = iota((8, LANES), 1)
    shift = lane % W
    component = (lane // (blocks * W)) * chunks
    bands_per_step = max(1, 16 // rows)

    def step(index, carry):
        tiles = []
        for inner in range(bands_per_step):
            band = index * bands_per_step + inner
            at_lane = pl.ds(pl.multiple_of(band * LANES, LANES), LANES)
            for group in range(rows // 8):
                at_row = pl.ds(group * 8, 8)
                place = low_ref[at_row, at_lane] + shift
                lane_id = place % LANES
                chosen = high_ref[at_row, at_lane] + place // LANES + component
                tile = jnp.zeros((8, LANES), jnp.float32)
                for part in range(4):
                    for chunk in range(chunks):
                        start = pl.multiple_of(band * band_width + chunk * LANES, LANES)
                        values = spec_ref[part, at_row, pl.ds(start, LANES)]
                        moved = jnp.take_along_axis(values, lane_id, axis=1, mode="promise_in_bounds")
                        tile = jnp.where(chosen == part * chunks + chunk, moved, tile)
                tiles.append(tile)
        count = len(tiles) * 8
        out_ref[pl.ds(pl.multiple_of(index * count, count), count), :] = jnp.concatenate(tiles, axis=0).astype(jnp.bfloat16)
        return carry

    lax.fori_loop(0, bands // bands_per_step, step, 0)


def pick(me, offset_parts, spec, band_width):
    bands = len(offset_parts)
    rows = spec.shape[1]
    vmem = pl.BlockSpec(memory_space=pltpu.VMEM)
    return pl.pallas_call(
        functools.partial(pick_kernel, bands, rows, band_width),
        out_shape=jax.ShapeDtypeStruct((bands * rows, LANES), jnp.bfloat16),
        in_specs=[pl.BlockSpec(memory_space=pltpu.SMEM)] + [vmem] * (bands + 1),
        out_specs=vmem,
        scratch_shapes=[pltpu.VMEM((rows, bands * LANES), jnp.int32)] * 2,
        compiler_params=pltpu.CompilerParams(vmem_limit_bytes=32 * 1024 * 1024),
        cost_estimate=pl.CostEstimate(flops=10_000_000, bytes_accessed=4 * spec.size, transcendentals=0),
        name="pick",
    )(me, *offset_parts, spec)


def split(values, count):
    parts = []
    for _ in range(count):
        part = values.astype(jnp.bfloat16)
        parts.append(part)
        values = values - part.astype(jnp.float32)
    return parts


def prepare_kernel(durations_ref, starts_ref, antenna_ref, fractions_ref, mask_ref, weigh_ref, coef_ref, kernel_ref):
    rows = starts_ref.shape[0]
    count = durations_ref.shape[0]
    sfts = antenna_ref.shape[1]
    sft = iota((rows, sfts), 1)
    start = starts_ref[:, 0:1]
    after = sft >= start
    for j in range(count):
        inside = after & (sft < start + durations_ref[j])
        mask_ref[pl.ds(j * rows, rows), :] = jnp.where(inside, 1.0, 0.0).astype(jnp.bfloat16)
    antenna = antenna_ref[...]
    a1, a2, b1, b2 = (antenna[n : n + 1] for n in range(4))
    terms = jnp.concatenate([a1 * a1 + a2 * a2, b1 * b1 + b2 * b2, a1 * b1 + a2 * b2, jnp.zeros((5, sfts), jnp.float32)], axis=0)
    weights = sum(lax.dot_general(mask_ref[...], part, NT, preferred_element_type=jnp.float32) for part in split(terms, 3))
    wa, wb, wc = (weights[:, n : n + 1] for n in range(3))
    shape = (rows * count, LANES)
    late = iota(shape, 1) >= LANES // 2
    coef_ref[0] = jnp.broadcast_to(1.0 / wa, shape)
    coef_ref[1] = jnp.broadcast_to(wa / (wa * wb - wc * wc), shape)
    coef_ref[2] = jnp.where(late, jnp.broadcast_to(wc / wa, shape), 0.0)
    upright = jnp.transpose(jnp.concatenate([antenna, jnp.zeros((LANES - 4, sfts), jnp.float32)], axis=0))
    shape = (sfts, LANES)
    late = iota(shape, 1) >= LANES // 2
    weigh_ref[0] = jnp.where(late, upright[:, 3:4], upright[:, 0:1])
    weigh_ref[1] = jnp.where(late, upright[:, 2:3], upright[:, 1:2])
    fractions = fractions_ref[...]
    templates = fractions.shape[1]
    blocks = kernel_ref.shape[1] // (4 * LANES)
    bin_id = iota((W, templates), 0)
    distance = fractions + (W // 2 - 1) - bin_id.astype(jnp.float32)
    alternate = 1.0 - 2.0 * (bin_id % 2).astype(jnp.float32)
    values = (alternate * jnp.sin(jnp.pi * fractions) / (jnp.pi * distance)).astype(jnp.bfloat16)
    kernel_ref[...] = jnp.zeros_like(kernel_ref)
    for part in range(2):
        for c in range(4):
            for b in range(blocks):
                row = ((part * 4 + c) * blocks + b) * W
                column = (c * blocks + b) * LANES
                kernel_ref[pl.ds(row, W), pl.ds(column, LANES)] = values[:, b * LANES : (b + 1) * LANES]


def prepare(durations, starts, antenna, fractions):
    count, rows, sfts = durations.shape[0], starts.shape[0], antenna.shape[0]
    columns = 4 * fractions.shape[0]
    features = 4 * W * (fractions.shape[0] // LANES)
    vmem = pl.BlockSpec(memory_space=pltpu.VMEM)
    return pl.pallas_call(
        prepare_kernel,
        out_shape=(
            jax.ShapeDtypeStruct((count * rows, sfts), jnp.bfloat16),
            jax.ShapeDtypeStruct((2, sfts, LANES), jnp.float32),
            jax.ShapeDtypeStruct((3, count * rows, LANES), jnp.float32),
            jax.ShapeDtypeStruct((2 * features, columns), jnp.bfloat16),
        ),
        in_specs=[pl.BlockSpec(memory_space=pltpu.SMEM), vmem, vmem, vmem],
        out_specs=(vmem,) * 4,
        compiler_params=pltpu.CompilerParams(vmem_limit_bytes=32 * 1024 * 1024),
        cost_estimate=pl.CostEstimate(flops=100_000_000, bytes_accessed=4_000_000, transcendentals=0),
        name="prepare",
    )(durations, jnp.broadcast_to(starts[:, None], (rows, LANES)), antenna.T, fractions[None, :])


def statistic_kernel(windows_ref, mask_ref, weigh_ref, coef_ref, kernel_ref, map_ref, loudest_ref):
    values = windows_ref[...].astype(jnp.float32)
    half = LANES // 2
    weighted = (weigh_ref[0] * values + weigh_ref[1] * pltpu.roll(values, half, 1)).astype(jnp.bfloat16)
    templates = map_ref.shape[1]
    rows = loudest_ref.shape[1]
    per_step = LANES // rows
    for step in range(map_ref.shape[0] // LANES):
        here = pl.ds(step * LANES, LANES)
        sums = jnp.dot(mask_ref[here, :], weighted, preferred_element_type=jnp.float32)
        sums = sums - coef_ref[2, here, :] * pltpu.roll(sums, half, 1)
        parts = jnp.concatenate(split(sums, 2), axis=1)
        found = jnp.dot(parts, kernel_ref[...], preferred_element_type=jnp.float32)
        ra, ia, rb, ib = (found[:, c * templates : (c + 1) * templates] for c in range(4))
        power_a, power_b = ra * ra + ia * ia, rb * rb + ib * ib
        best = None
        for b in range(templates // LANES):
            columns = slice(b * LANES, (b + 1) * LANES)
            result = coef_ref[0, here, :] * power_a[:, columns] + coef_ref[1, here, :] * power_b[:, columns]
            map_ref[here, columns] = result
            best = result if best is None else jnp.maximum(best, result)
        best = jnp.max(jnp.transpose(best), axis=0, keepdims=True)
        for n in range(per_step):
            turned = best if n == 0 else pltpu.roll(best, LANES - n * rows, 1)
            loudest_ref[pl.ds(step * per_step + n, 1), :] = turned[:, :rows]


def statistic(windows, mask, weigh, coef, kernel, rows):
    count = mask.shape[0] // rows
    templates = kernel.shape[1] // 4
    vmem = pl.BlockSpec(memory_space=pltpu.VMEM)
    return pl.pallas_call(
        statistic_kernel,
        out_shape=(
            jax.ShapeDtypeStruct((count * rows, templates), jnp.float32),
            jax.ShapeDtypeStruct((count, rows), jnp.float32),
        ),
        in_specs=[vmem] * 5,
        out_specs=(vmem, vmem),
        compiler_params=pltpu.CompilerParams(vmem_limit_bytes=32 * 1024 * 1024),
        cost_estimate=pl.CostEstimate(flops=400_000_000, bytes_accessed=4_000_000, transcendentals=0),
        name="statistic",
    )(windows, mask, weigh, coef, kernel)


def to_all(values, axis):
    size = lax.axis_size(axis)
    return [values] + [lax.ppermute(values, axis, [(n, n ^ r) for n in range(size)]) for r in range(1, size)]


def body(spectra, offsets, fractions, antenna, starts, durations):
    bands, cores = lax.axis_size("tmpl"), lax.axis_size("tm")
    sft_rows = spectra.shape[0]
    band_width = spectra.shape[2] // bands
    grid_size = starts.shape[0]
    my_rows = grid_size // cores
    me = lax.axis_index("tmpl").astype(jnp.int32)[None]
    offset_parts = to_all(offsets.T, "tmpl")
    spec = jnp.transpose(spectra, (1, 0, 2)).astype(jnp.float32)
    my_durations = lax.dynamic_slice_in_dim(durations, lax.axis_index("tm") * my_rows, my_rows, 0)
    prepared = prepare(my_durations, starts, antenna, fractions)
    windows = pick(me, offset_parts, spec, band_width).reshape(1, bands, sft_rows, LANES)
    windows = jnp.broadcast_to(windows, (cores, bands, sft_rows, LANES)).reshape(cores * bands, sft_rows, LANES)
    arrived = lax.all_to_all(windows, ("tm", "tmpl"), split_axis=0, concat_axis=0, tiled=True)
    arrived = arrived.reshape(cores * bands * sft_rows, LANES)
    fstat_map, loudest = statistic(arrived, *prepared, grid_size)
    loudest = functools.reduce(jnp.maximum, to_all(loudest, "tmpl"))
    return (fstat_map.reshape(my_rows, grid_size, -1), loudest)


def solution(mesh):
    in_specs = (
        P(("grp", "tm", "tmpl"), None, None),
        P(("grp", "tm"), "tmpl"),
        P(("grp", "tmpl")),
        P("grp", None),
        P("grp"),
        P("grp"),
    )
    out_specs = (P("tm", None, ("grp", "tmpl")), P(("grp", "tm"), None))
    return jax.shard_map(body, mesh=mesh, in_specs=in_specs, out_specs=out_specs, check_vma=False)
```

time: 117 us -> 52.4 us (0.45)
  blocking collectives: 22.5 us -> 0 us
  other arithmetic: 24.5 us -> 5.35 us
  starting transfers between devices: 10.7 us -> 28 us
  between operations: 14.2 us -> 0.71 us
  local copies, waits for them, and re-layouts: 15.1 us -> 3.03 us
  matrix products: 11.9 us -> 0 us
  waiting for transfers between devices: 17.6 us -> 8.97 us
  Pallas kernels: 0 us -> 6.03 us
    ppermute x0 -> x14, starting transfers between devices: none -> 23.6 us  [to_all(): lax.ppermute(values, axis, [(n, n ^ r) for n in range(size)])]
    pmax x1 -> x0, blocking collectives: 22.5 us -> none  [body(): loudest = lax.pmax(jnp.max(fstat_map, axis=2), 'tmpl')]
    reduce_max x1 -> x0, other arithmetic: 12.7 us -> none  [body(): loudest = lax.pmax(jnp.max(fstat_map, axis=2), 'tmpl')]
    dot_general x4 -> x0, matrix products: 11.9 us -> none  [the longest x1 7.05 us: body(): jnp.einsum('sctn,stkn->stck', split_bands, picker, preferred_element_type...]
    add x5 -> x0, other arithmetic: 7.51 us -> none  [the longest x1 6.67 us: statistic(): real_a * real_a + imag_a * imag_a]
    all_to_all x2 -> x1, starting transfers between devices: 10.6 us -> 4.39 us  [body(): lax.all_to_all(windows, ('tm', 'tmpl'), split_axis=0, concat_axis=0, tile...]
    all_to_all x2 -> x1, waiting for transfers between devices: 11.6 us -> 5.54 us  [body(): lax.all_to_all(windows, ('tm', 'tmpl'), split_axis=0, concat_axis=0, tile...]
    pallas_call x0 -> x3, Pallas kernels: none -> 6.03 us  [the longest x1 2.15 us: statistic(): pl.pallas_call(statistic_kernel, out_shape=(jax.ShapeDtypeStruct((count *...]
  transfers between devices with their start and end apart: 3 -> 15, of which waited for: 3 -> 5; matrix products, arithmetic and copies ran while one was open for 5% -> 9% of each run, Pallas kernels for 0% -> 4%
where the time goes in v1:
time: 52.4 us; the launch traced here: 52.1 us
  starting transfers between devices  28 us (53%)
  waiting for transfers between devices  8.97 us (17%)
  Pallas kernels  6.03 us (12%)
  other arithmetic  5.35 us (10%)
  local copies, waits for them, and re-layouts  3.03 us (6%)
  between operations  0.71 us (1%)
    ppermute x14, starting transfers between devices, to_all(): lax.ppermute(values, axis, [(n, n ^ r) for n in range(size)])  23.6 us
    all_to_all x1, waiting for transfers between devices, body(): lax.all_to_all(windows, ('tm', 'tmpl'), split_axis=0, concat_axis=0, tile...  5.54 us
    convert_element_type x1, other arithmetic, body(): spec = jnp.transpose(spectra, (1, 0, 2)).astype(jnp.float32)  4.75 us
    all_to_all x1, starting transfers between devices, body(): lax.all_to_all(windows, ('tm', 'tmpl'), split_axis=0, concat_axis=0, tile...  4.39 us
    ppermute x14, waiting for transfers between devices, to_all(): lax.ppermute(values, axis, [(n, n ^ r) for n in range(size)])  3.44 us
    unnamed x12, local copies, waits for them, and re-layouts  2.21 us
    pallas_call x1, Pallas kernels, statistic(): pl.pallas_call(statistic_kernel, out_shape=(jax.ShapeDtypeStruct((count *...  2.15 us
    pallas_call x1, Pallas kernels, prepare(): pl.pallas_call(prepare_kernel, out_shape=(jax.ShapeDtypeStruct((count * r...  1.96 us
  transfers between devices with their start and end apart: 15, of which 5 were waited for; matrix products, arithmetic and copies ran while one was open for 9% of the time, Pallas kernels for 4%

profile of v1, /device:TPU:0, one launch (start us, length us, event | category | flops | bytes accessed | tf_op | source)
XLA Modules:
  0.0 52.1 jit_solution(17912578339094040421)
XLA Ops:
  0.6 3.0 %collective-permute-start = (s32[2,256]{1,0:T(2,128)}, s32[2,256]{1,0:T(2,128)S(1)}, u32[]{:S(2)}, u32[]{:S(2)}) collective-permute-start(s32[2,256]{1,0:T(2,128)} %bitcast.12), channel_id=1, source_target_pairs={{0,2},{2,0},{4,6},{6,4},{8,10},{10,8},{12,14},{14,12},{1,3},{3,1},... | collective-permute-start | bytes 6152 | tf_op jit(solution)/shard_map/ppermute | solution.py:206
  3.7 1.6 %collective-permute-start.1 = (s32[2,256]{1,0:T(2,128)}, s32[2,256]{1,0:T(2,128)S(1)}, u32[]{:S(2)}, u32[]{:S(2)}) collective-permute-start(s32[2,256]{1,0:T(2,128)} %bitcast.13), channel_id=1, source_target_pairs={{0,4},{2,6},{4,0},{6,2},{8,12},{10,14},{12,8},{14,10},{1,5},{3,7},... | collective-permute-start | bytes 6152 | tf_op jit(solution)/shard_map/ppermute | solution.py:206
  5.3 3.0 %collective-permute-start.3 = (s32[2,256]{1,0:T(2,128)}, s32[2,256]{1,0:T(2,128)S(1)}, u32[]{:S(2)}, u32[]{:S(2)}) collective-permute-start(s32[2,256]{1,0:T(2,128)} %bitcast.15), channel_id=1, source_target_pairs={{0,8},{2,10},{4,12},{6,14},{8,0},{10,2},{12,4},{14,6},{1,9},{3,11}... | collective-permute-start | bytes 6152 | tf_op jit(solution)/shard_map/ppermute | solution.py:206
  8.2 1.3 %collective-permute-start.4 = (s32[2,256]{1,0:T(2,128)}, s32[2,256]{1,0:T(2,128)S(1)}, u32[]{:S(2)}, u32[]{:S(2)}) collective-permute-start(s32[2,256]{1,0:T(2,128)} %bitcast.16), channel_id=1, source_target_pairs={{0,10},{2,8},{4,14},{6,12},{8,2},{10,0},{12,6},{14,4},{1,11},{3,9}... | collective-permute-start | bytes 6152 | tf_op jit(solution)/shard_map/ppermute | solution.py:206
  9.5 3.6 %collective-permute-start.5 = (s32[2,256]{1,0:T(2,128)}, s32[2,256]{1,0:T(2,128)S(1)}, u32[]{:S(2)}, u32[]{:S(2)}) collective-permute-start(s32[2,256]{1,0:T(2,128)} %bitcast.17), channel_id=1, source_target_pairs={{0,12},{2,14},{4,8},{6,10},{8,4},{10,6},{12,0},{14,2},{1,13},{3,15... | collective-permute-start | bytes 6152 | tf_op jit(solution)/shard_map/ppermute | solution.py:206
  13.1 4.7 %convert_bitcast_fusion.refs_8_ = f32[4,32,8192]{2,1,0:T(8,128)} fusion(bf16[32,4,8192]{2,1,0:T(4,128)(2,1)} %param.6), kind=kLoop, calls=%fused_computation | loop fusion | flops 1048576 | bytes 6291456 | tf_op jit(solution)/shard_map/convert_element_type | solution.py:217
  17.9 1.7 %collective-permute-done.6.refs_7_ = s32[2,256]{1,0:T(2,128)S(1)} collective-permute-done((s32[2,256]{1,0:T(2,128)}, s32[2,256]{1,0:T(2,128)S(1)}, u32[]{:S(2)}, u32[]{:S(2)}) %collective-permute-start.6) | collective-permute-done | bytes 2080 | tf_op jit(solution)/shard_map/ppermute | solution.py:206
  19.6 2.2 %copy-done = f32[4,32,8192]{2,1,0:T(8,128)S(1)} copy-done((f32[4,32,8192]{2,1,0:T(8,128)S(1)}, f32[4,32,8192]{2,1,0:T(8,128)}, u32[]{:S(2)}) %copy-start) | copy-done | bytes 4194328
  21.8 1.9 %pick.1 = bf16[256,128]{1,0:T(8,128)(2,1)S(1)} custom-call(s32[1]{0:T(128)} %bitcast.me_ref, s32[2,256]{1,0:T(2,128)S(1)} %bitcast.19, s32[2,256]{1,0:T(2,128)S(1)} %collective-permute-done.refs_1_, s32[2,256]{1,0:T(2,128)S(1)} %collective-permute-done.1.refs_2_, s32[2,256]{1,0:T(2,128)S(1)} %collective-permute-done.2.refs_3_, ...), custom_call_target="tpu_custom_call" | custom-call | flops 10000000 | bytes 4194304 | tf_op jit(solution)/shard_map/pick/pallas_call | solution.py:76
  23.8 0.7 %broadcast_in_dim.21 = bf16[2,8,32,128]{3,2,1,0:T(8,128)(2,1)} broadcast(bf16[8,32,128]{2,1,0:T(8,128)(2,1)S(1)} %bitcast.11), dimensions={1,2,3} | broadcast | bytes 196608 | tf_op jit(solution)/shard_map/broadcast_in_dim | solution.py:221
  24.4 4.4 %all-to-all-start = ((bf16[16,32,128]{2,1,0:T(8,128)(2,1)}), bf16[16,32,128]{2,1,0:T(8,128)(2,1)S(1)}, u32[]{:S(2)}, u32[]{:S(2)}) async-start(bf16[16,32,128]{2,1,0:T(8,128)(2,1)} %bitcast.4), calls=%async_computation | async-start | bytes 262144 | tf_op jit(solution)/shard_map/all_to_all | solution.py:222
  29.0 2.0 %prepare.1 = (bf16[512,512]{1,0:T(8,128)(2,1)S(1)}, f32[2,512,128]{2,1,0:T(8,128)S(1)}, f32[3,512,128]{2,1,0:T(8,128)S(1)}, bf16[256,1024]{1,0:T(8,128)(2,1)S(1)}) custom-call(s32[16]{0:T(128)S(1)} %dynamic_slice.3.durations_ref, s32[32,128]{1,0:T(8,128)S(1)} %broadcast_in_dim.22.starts_ref, f32[4,512]{1,0:T(4,128)S(1)} %bitcast.20, f32[1,256]{1,0:T(1,128)S(1)} %bitcast.21), custom_call_target="tpu_custom_call" | custom-call | flops 100000000 | bytes 4000000 | tf_op jit(solution)/shard_map/prepare/pallas_call | solution.py:143
  31.0 5.5 %all-to-all-done = bf16[16,32,128]{2,1,0:T(8,128)(2,1)S(1)} async-done(((bf16[16,32,128]{2,1,0:T(8,128)(2,1)}), bf16[16,32,128]{2,1,0:T(8,128)(2,1)S(1)}, u32[]{:S(2)}, u32[]{:S(2)}) %all-to-all-start) | async-done | bytes 131104 | tf_op jit(solution)/shard_map/all_to_all | solution.py:222
  36.5 2.2 %statistic.1 = (f32[512,256]{1,0:T(8,128)}, f32[16,32]{1,0:T(8,128)S(1)}) custom-call(bf16[512,128]{1,0:T(8,128)(2,1)S(1)} %bitcast.10, bf16[512,512]{1,0:T(8,128)(2,1)S(1)} %get-tuple-element.8.mask_ref, f32[2,512,128]{2,1,0:T(8,128)S(1)} %get-tuple-element.9.weigh_ref, f32[3,512,128]{2,1,0:T(8,128)S(1)} %get-tuple-element.10.coef_ref, ...), custom_call_target="tpu_custom_call" | custom-call | flops 400000000 | bytes 4000000 | tf_op jit(solution)/shard_map/statistic/pallas_call | solution.py:190
  38.7 0.7 %collective-permute-start.10 = (f32[16,32]{1,0:T(8,128)S(1)}, f32[16,32]{1,0:T(8,128)S(1)}, u32[]{:S(2)}, u32[]{:S(2)}) collective-permute-start(f32[16,32]{1,0:T(8,128)S(1)} %get-tuple-element.13), channel_id=1, source_target_pairs={{0,8},{2,10},{4,12},{6,14},{8,0},{10,2},{12,4},{14,6},{1,9},{3,11}... | collective-permute-start | bytes 6152 | tf_op jit(solution)/shard_map/ppermute | solution.py:206
  39.4 2.2 %collective-permute-start.11 = (f32[16,32]{1,0:T(8,128)S(1)}, f32[16,32]{1,0:T(8,128)S(1)}, u32[]{:S(2)}, u32[]{:S(2)}) collective-permute-start(f32[16,32]{1,0:T(8,128)S(1)} %get-tuple-element.13), channel_id=1, source_target_pairs={{0,10},{2,8},{4,14},{6,12},{8,2},{10,0},{12,6},{14,4},{1,11},{3,9}... | collective-permute-start | bytes 6152 | tf_op jit(solution)/shard_map/ppermute | solution.py:206
  41.6 1.0 %collective-permute-start.12 = (f32[16,32]{1,0:T(8,128)S(1)}, f32[16,32]{1,0:T(8,128)S(1)}, u32[]{:S(2)}, u32[]{:S(2)}) collective-permute-start(f32[16,32]{1,0:T(8,128)S(1)} %get-tuple-element.13), channel_id=1, source_target_pairs={{0,12},{2,14},{4,8},{6,10},{8,4},{10,6},{12,0},{14,2},{1,13},{3,15... | collective-permute-start | bytes 6152 | tf_op jit(solution)/shard_map/ppermute | solution.py:206
  42.6 3.7 %collective-permute-start.13 = (f32[16,32]{1,0:T(8,128)S(1)}, f32[16,32]{1,0:T(8,128)S(1)}, u32[]{:S(2)}, u32[]{:S(2)}) collective-permute-start(f32[16,32]{1,0:T(8,128)S(1)} %get-tuple-element.13), channel_id=1, source_target_pairs={{0,14},{2,12},{4,10},{6,8},{8,6},{10,4},{12,2},{14,0},{1,15},{3,13... | collective-permute-start | bytes 6152 | tf_op jit(solution)/shard_map/ppermute | solution.py:206
  46.3 0.6 %collective-permute-start.7 = (f32[16,32]{1,0:T(8,128)S(1)}, f32[16,32]{1,0:T(8,128)S(1)}, u32[]{:S(2)}, u32[]{:S(2)}) collective-permute-start(f32[16,32]{1,0:T(8,128)S(1)} %get-tuple-element.13), channel_id=1, source_target_pairs={{0,2},{2,0},{4,6},{6,4},{8,10},{10,8},{12,14},{14,12},{1,3},{3,1},... | collective-permute-start | bytes 6152 | tf_op jit(solution)/shard_map/ppermute | solution.py:206
  46.9 2.9 %collective-permute-start.9 = (f32[16,32]{1,0:T(8,128)S(1)}, f32[16,32]{1,0:T(8,128)S(1)}, u32[]{:S(2)}, u32[]{:S(2)}) collective-permute-start(f32[16,32]{1,0:T(8,128)S(1)} %get-tuple-element.13), channel_id=1, source_target_pairs={{0,6},{2,4},{4,2},{6,0},{8,14},{10,12},{12,10},{14,8},{1,7},{3,5},... | collective-permute-start | bytes 6152 | tf_op jit(solution)/shard_map/ppermute | solution.py:206
  49.8 0.1 collective-permute-done.7
  50.0 0.6 %collective-permute-done.8 = f32[16,32]{1,0:T(8,128)S(1)} collective-permute-done((f32[16,32]{1,0:T(8,128)S(1)}, f32[16,32]{1,0:T(8,128)S(1)}, u32[]{:S(2)}, u32[]{:S(2)}) %collective-permute-start.8) | collective-permute-done | bytes 2080 | tf_op jit(solution)/shard_map/ppermute | solution.py:206
  50.5 1.0 %collective-permute-done.9 = f32[16,32]{1,0:T(8,128)S(1)} collective-permute-done((f32[16,32]{1,0:T(8,128)S(1)}, f32[16,32]{1,0:T(8,128)S(1)}, u32[]{:S(2)}, u32[]{:S(2)}) %collective-permute-start.9) | collective-permute-done | bytes 2080 | tf_op jit(solution)/shard_map/ppermute | solution.py:206
  51.5 0.6 %maximum_maximum_fusion = f32[16,32]{1,0:T(8,128)} fusion(f32[16,32]{1,0:T(8,128)S(1)} %collective-permute-done.13, f32[16,32]{1,0:T(8,128)S(1)} %collective-permute-done.12, f32[16,32]{1,0:T(8,128)S(1)} %collective-permute-done.11, f32[16,32]{1,0:T(8,128)S(1)} %collective-permute-done.10, f32[16,32]{1,0:T(8,128)S(1)} %collective-permute-done.9, ...), kind=kLoop, calls=%fused_computation.1 | loop fusion | flops 3584 | bytes 18432 | tf_op jit(solution)/shard_map/max | solution.py:225
  (26 shorter events, 0.2 us)
Async XLA Ops:
  0.6 19.0 %copy-start.1 = (s32[256,2]{0,1:T(2,128)S(1)}, s32[256,2]{0,1:T(2,128)}, u32[]{:S(2)}) copy-start(s32[256,2]{0,1:T(2,128)} %param.7) | copy-start | bytes 6148
  0.6 8.9 %collective-permute-start = (s32[2,256]{1,0:T(2,128)}, s32[2,256]{1,0:T(2,128)S(1)}, u32[]{:S(2)}, u32[]{:S(2)}) collective-permute-start(s32[2,256]{1,0:T(2,128)} %bitcast.12), channel_id=1, source_target_pairs={{0,2},{2,0},{4,6},{6,4},{8,10},{10,8},{12,14},{14,12},{1,3},{3,1},... | collective-permute-start | bytes 6152 | tf_op jit(solution)/shard_map/ppermute | solution.py:206
  3.7 9.5 %collective-permute-start.1 = (s32[2,256]{1,0:T(2,128)}, s32[2,256]{1,0:T(2,128)S(1)}, u32[]{:S(2)}, u32[]{:S(2)}) collective-permute-start(s32[2,256]{1,0:T(2,128)} %bitcast.13), channel_id=1, source_target_pairs={{0,4},{2,6},{4,0},{6,2},{8,12},{10,14},{12,8},{14,10},{1,5},{3,7},... | collective-permute-start | bytes 6152 | tf_op jit(solution)/shard_map/ppermute | solution.py:206
  5.2 12.6 %collective-permute-start.2 = (s32[2,256]{1,0:T(2,128)}, s32[2,256]{1,0:T(2,128)S(1)}, u32[]{:S(2)}, u32[]{:S(2)}) collective-permute-start(s32[2,256]{1,0:T(2,128)} %bitcast.14), channel_id=1, source_target_pairs={{0,6},{2,4},{4,2},{6,0},{8,14},{10,12},{12,10},{14,8},{1,7},{3,5},... | collective-permute-start | bytes 6152 | tf_op jit(solution)/shard_map/ppermute | solution.py:206
  5.3 12.6 %collective-permute-start.3 = (s32[2,256]{1,0:T(2,128)}, s32[2,256]{1,0:T(2,128)S(1)}, u32[]{:S(2)}, u32[]{:S(2)}) collective-permute-start(s32[2,256]{1,0:T(2,128)} %bitcast.15), channel_id=1, source_target_pairs={{0,8},{2,10},{4,12},{6,14},{8,0},{10,2},{12,4},{14,6},{1,9},{3,11}... | collective-permute-start | bytes 6152 | tf_op jit(solution)/shard_map/ppermute | solution.py:206
  8.2 9.7 %collective-permute-start.4 = (s32[2,256]{1,0:T(2,128)}, s32[2,256]{1,0:T(2,128)S(1)}, u32[]{:S(2)}, u32[]{:S(2)}) collective-permute-start(s32[2,256]{1,0:T(2,128)} %bitcast.16), channel_id=1, source_target_pairs={{0,10},{2,8},{4,14},{6,12},{8,2},{10,0},{12,6},{14,4},{1,11},{3,9}... | collective-permute-start | bytes 6152 | tf_op jit(solution)/shard_map/ppermute | solution.py:206
  9.5 8.4 %collective-permute-start.5 = (s32[2,256]{1,0:T(2,128)}, s32[2,256]{1,0:T(2,128)S(1)}, u32[]{:S(2)}, u32[]{:S(2)}) collective-permute-start(s32[2,256]{1,0:T(2,128)} %bitcast.17), channel_id=1, source_target_pairs={{0,12},{2,14},{4,8},{6,10},{8,4},{10,6},{12,0},{14,2},{1,13},{3,15... | collective-permute-start | bytes 6152 | tf_op jit(solution)/shard_map/ppermute | solution.py:206
  13.1 6.5 %collective-permute-start.6 = (s32[2,256]{1,0:T(2,128)}, s32[2,256]{1,0:T(2,128)S(1)}, u32[]{:S(2)}, u32[]{:S(2)}) collective-permute-start(s32[2,256]{1,0:T(2,128)} %bitcast.18), channel_id=1, source_target_pairs={{0,14},{2,12},{4,10},{6,8},{8,6},{10,4},{12,2},{14,0},{1,15},{3,13... | collective-permute-start | bytes 6152 | tf_op jit(solution)/shard_map/ppermute | solution.py:206
  19.6 2.2 %copy-start = (f32[4,32,8192]{2,1,0:T(8,128)S(1)}, f32[4,32,8192]{2,1,0:T(8,128)}, u32[]{:S(2)}) copy-start(f32[4,32,8192]{2,1,0:T(8,128)} %convert_bitcast_fusion.refs_8_) | copy-start | bytes 12582916
  21.8 7.0 %copy-start.5 = (s32[32]{0:T(128)S(1)}, s32[32]{0:T(128)}, u32[]{:S(2)}) copy-start(s32[32]{0:T(128)} %param.11) | copy-start | bytes 388
  21.8 7.1 %copy-start.4 = (s32[32]{0:T(128)S(1)}, s32[32]{0:T(128)}, u32[]{:S(2)}) copy-start(s32[32]{0:T(128)} %param.10) | copy-start | bytes 388
  21.8 7.2 %copy-start.2 = (f32[512,4]{0,1:T(4,128)S(1)}, f32[512,4]{0,1:T(4,128)}, u32[]{:S(2)}) copy-start(f32[512,4]{0,1:T(4,128)} %param.9) | copy-start | bytes 24580
  21.8 7.2 %copy-start.3 = (f32[256]{0:T(256)S(1)}, f32[256]{0:T(256)}, u32[]{:S(2)}) copy-start(f32[256]{0:T(256)} %param.8) | copy-start | bytes 3076
  24.4 12.1 %all-to-all-start = ((bf16[16,32,128]{2,1,0:T(8,128)(2,1)}), bf16[16,32,128]{2,1,0:T(8,128)(2,1)S(1)}, u32[]{:S(2)}, u32[]{:S(2)}) async-start(bf16[16,32,128]{2,1,0:T(8,128)(2,1)} %bitcast.4), calls=%async_computation | async-start | bytes 262144 | tf_op jit(solution)/shard_map/all_to_all | solution.py:222
  38.7 8.2 %collective-permute-start.10 = (f32[16,32]{1,0:T(8,128)S(1)}, f32[16,32]{1,0:T(8,128)S(1)}, u32[]{:S(2)}, u32[]{:S(2)}) collective-permute-start(f32[16,32]{1,0:T(8,128)S(1)} %get-tuple-element.13), channel_id=1, source_target_pairs={{0,8},{2,10},{4,12},{6,14},{8,0},{10,2},{12,4},{14,6},{1,9},{3,11}... | collective-permute-start | bytes 6152 | tf_op jit(solution)/shard_map/ppermute | solution.py:206
  39.4 7.5 %collective-permute-start.11 = (f32[16,32]{1,0:T(8,128)S(1)}, f32[16,32]{1,0:T(8,128)S(1)}, u32[]{:S(2)}, u32[]{:S(2)}) collective-permute-start(f32[16,32]{1,0:T(8,128)S(1)} %get-tuple-element.13), channel_id=1, source_target_pairs={{0,10},{2,8},{4,14},{6,12},{8,2},{10,0},{12,6},{14,4},{1,11},{3,9}... | collective-permute-start | bytes 6152 | tf_op jit(solution)/shard_map/ppermute | solution.py:206
  41.6 8.2 %collective-permute-start.12 = (f32[16,32]{1,0:T(8,128)S(1)}, f32[16,32]{1,0:T(8,128)S(1)}, u32[]{:S(2)}, u32[]{:S(2)}) collective-permute-start(f32[16,32]{1,0:T(8,128)S(1)} %get-tuple-element.13), channel_id=1, source_target_pairs={{0,12},{2,14},{4,8},{6,10},{8,4},{10,6},{12,0},{14,2},{1,13},{3,15... | collective-permute-start | bytes 6152 | tf_op jit(solution)/shard_map/ppermute | solution.py:206
  42.6 7.2 %collective-permute-start.13 = (f32[16,32]{1,0:T(8,128)S(1)}, f32[16,32]{1,0:T(8,128)S(1)}, u32[]{:S(2)}, u32[]{:S(2)}) collective-permute-start(f32[16,32]{1,0:T(8,128)S(1)} %get-tuple-element.13), channel_id=1, source_target_pairs={{0,14},{2,12},{4,10},{6,8},{8,6},{10,4},{12,2},{14,0},{1,15},{3,13... | collective-permute-start | bytes 6152 | tf_op jit(solution)/shard_map/ppermute | solution.py:206
  46.3 3.7 %collective-permute-start.7 = (f32[16,32]{1,0:T(8,128)S(1)}, f32[16,32]{1,0:T(8,128)S(1)}, u32[]{:S(2)}, u32[]{:S(2)}) collective-permute-start(f32[16,32]{1,0:T(8,128)S(1)} %get-tuple-element.13), channel_id=1, source_target_pairs={{0,2},{2,0},{4,6},{6,4},{8,10},{10,8},{12,14},{14,12},{1,3},{3,1},... | collective-permute-start | bytes 6152 | tf_op jit(solution)/shard_map/ppermute | solution.py:206
  46.9 3.7 %collective-permute-start.8 = (f32[16,32]{1,0:T(8,128)S(1)}, f32[16,32]{1,0:T(8,128)S(1)}, u32[]{:S(2)}, u32[]{:S(2)}) collective-permute-start(f32[16,32]{1,0:T(8,128)S(1)} %get-tuple-element.13), channel_id=1, source_target_pairs={{0,4},{2,6},{4,0},{6,2},{8,12},{10,14},{12,8},{14,10},{1,5},{3,7},... | collective-permute-start | bytes 6152 | tf_op jit(solution)/shard_map/ppermute | solution.py:206
  46.9 4.6 %collective-permute-start.9 = (f32[16,32]{1,0:T(8,128)S(1)}, f32[16,32]{1,0:T(8,128)S(1)}, u32[]{:S(2)}, u32[]{:S(2)}) collective-permute-start(f32[16,32]{1,0:T(8,128)S(1)} %get-tuple-element.13), channel_id=1, source_target_pairs={{0,6},{2,4},{4,2},{6,0},{8,14},{10,12},{12,10},{14,8},{1,7},{3,5},... | collective-permute-start | bytes 6152 | tf_op jit(solution)/shard_map/ppermute | solution.py:206
